TPU v7x, 32 devices: a whole 2x2x4 slice. The times are simulated.
32 devices in a mesh: dom: 2 (over x), space: 16 (over z, y, core).
Axes of the slice: x: 2, y: 2, z: 4, core: 2. Of those that a mesh axis runs over, the one named last changes fastest.
Arguments:
- inputs: bfloat16 [2, 32, 2048, 2048], P('dom', None, 'space'), parts along dimension 0, may hold values from -10.5 to 10.5
- target: bfloat16 [2, 32, 2048, 2048], P('dom', None, 'space'), parts along dimension 0, may hold values from -6 to 6
- spectral_weight: float32 [64, 32, 32, 128], P('space'), may hold values from -18 to 18
- local_weight: bfloat16 [32, 32], replicated, may hold values from -1 to 1
- bias_term: float32 [32], replicated, may hold values from -3 to 3
Outputs:
- grad_input: bfloat16 [2, 32, 2048, 2048], P('dom', None, 'space'), parts along dimension 0
- grad_spectral: float32 [64, 64, 32, 128], P('space', 'dom'), parts along dimension 1
- grad_local: float32 [64, 32], P('dom'), parts along dimension 0
- grad_bias: float32 [64], P('dom'), parts along dimension 0
There are 2 independent parts, one for each index of `dom`. A program takes and returns all parts, laid end to end along the dimension named above; an argument that names none is the same for every part. Nothing has to cross between parts.
All inputs are finite; a program needn't handle non-finite values.
Results may differ from a plain program's by a relative error of at most 0.014.
Values may be sent and summed in bfloat16 or wider, within the bound.
No kernel may reach another device: no remote copies, remote signals or barrier semaphores. Data moves between devices by JAX's collectives and lax.ppermute only.
A program may use at most 192 MiB of HBM per device.

v0:
```python
import math

import jax
import jax.numpy as jnp
from jax import lax
from jax.sharding import PartitionSpec as P

H = 2048
W = 2048
KX = 64
KY = 64


PRECISE = lax.Precision.HIGHEST


def row_table():
    mode_index = jnp.arange(KY, dtype=jnp.int32)[:, None]
    column = jnp.arange(W, dtype=jnp.int32)[None, :]
    angles = (mode_index * column % W).astype(jnp.float32) * (2.0 * math.pi / W)
    factor = 1.0 / math.sqrt(H * W)
    return jnp.stack([jnp.cos(angles) * factor, -jnp.sin(angles) * factor]).astype(jnp.bfloat16)


def column_table(row_index):
    column = jnp.arange(KX, dtype=jnp.int32)
    frequency = jnp.where(column < KX // 2, column, column + H - KX)
    angles = (row_index[:, None] * frequency[None, :] % H).astype(jnp.float32) * (2.0 * math.pi / H)
    return jnp.concatenate([jnp.cos(angles), jnp.sin(angles)], axis=1)


def mode_weights(start_mode, mode_count):
    mode_index = start_mode + jnp.arange(mode_count, dtype=jnp.int32)
    return jnp.where(mode_index == 0, 1.0, 2.0).astype(jnp.float32)


def row_analysis(field_data, basis):
    return jnp.einsum("schw,pkw->kpsch", field_data, basis, preferred_element_type=jnp.float32)


def row_synth(spectra, basis):
    return jnp.einsum("kpsch,pkw->schw", spectra, basis, preferred_element_type=jnp.float32)


def column_modes(slab_part, basis):
    product = jnp.einsum("kpsch,hj->kpscj", slab_part, basis, precision=PRECISE)
    half_count = basis.shape[1] // 2
    real_part = product[:, 0, :, :, :half_count] + product[:, 1, :, :, half_count:]
    imag_part = product[:, 1, :, :, :half_count] - product[:, 0, :, :, half_count:]
    return jnp.concatenate([real_part, imag_part], axis=-1)


def column_synth(mode_data, basis):
    half_count = basis.shape[1] // 2
    real_part, imag_part = (mode_data[..., :half_count], mode_data[..., half_count:])
    cosines, sine_part = (basis[:, :half_count], basis[:, half_count:])
    first_part = jnp.einsum("ysok,hk->ysoh", real_part, cosines, precision=PRECISE) - jnp.einsum(
        "ysok,hk->ysoh", imag_part, sine_part, precision=PRECISE
    )
    second = jnp.einsum("ysok,hk->ysoh", real_part, sine_part, precision=PRECISE) + jnp.einsum(
        "ysok,hk->ysoh", imag_part, cosines, precision=PRECISE
    )
    return jnp.stack([first_part, second], axis=1).astype(jnp.bfloat16)


def split_complex(mode_data):
    half_count = mode_data.shape[-1] // 2
    return (mode_data[..., :half_count], mode_data[..., half_count:])


def mix_modes(input_modes, weight):
    spec_real, spec_imag = split_complex(input_modes)
    weight_real, weight_imag = split_complex(weight)
    form = "ysck,ycok->ysok"
    out_real = jnp.einsum(form, spec_real, weight_real, precision=PRECISE) - jnp.einsum(
        form, spec_imag, weight_imag, precision=PRECISE
    )
    out_imag = jnp.einsum(form, spec_real, weight_imag, precision=PRECISE) + jnp.einsum(
        form, spec_imag, weight_real, precision=PRECISE
    )
    return jnp.concatenate([out_real, out_imag], axis=-1)


def mix_back(delta_modes, weight):
    delta_real, delta_imag = split_complex(delta_modes)
    weight_real, weight_imag = split_complex(weight)
    form = "ysok,ycok->ysck"
    out_real = jnp.einsum(form, delta_real, weight_real, precision=PRECISE) + jnp.einsum(
        form, delta_imag, weight_imag, precision=PRECISE
    )
    out_imag = jnp.einsum(form, delta_imag, weight_real, precision=PRECISE) - jnp.einsum(
        form, delta_real, weight_imag, precision=PRECISE
    )
    return jnp.concatenate([out_real, out_imag], axis=-1)


def mix_grad(input_modes, delta_modes):
    spec_real, spec_imag = split_complex(input_modes)
    delta_real, delta_imag = split_complex(delta_modes)
    form = "ysck,ysok->ycok"
    grad_real = jnp.einsum(form, spec_real, delta_real, precision=PRECISE) + jnp.einsum(
        form, spec_imag, delta_imag, precision=PRECISE
    )
    grad_imag = jnp.einsum(form, spec_real, delta_imag, precision=PRECISE) - jnp.einsum(
        form, spec_imag, delta_real, precision=PRECISE
    )
    return jnp.concatenate([grad_real, grad_imag], axis=-1)


def gelu_parts(value):
    normal_cdf = 0.5 * (1.0 + jax.scipy.special.erf(value * (1.0 / math.sqrt(2.0))))
    density = jnp.exp(-0.5 * value * value) * (1.0 / math.sqrt(2.0 * math.pi))
    return (value * normal_cdf, normal_cdf + value * density)


def per_device(inputs, target, spectral_weight, local_weight, bias_term):
    mode_block = spectral_weight.shape[0]
    row_count = inputs.shape[2]
    device = lax.axis_index("space")
    row_basis = row_table()
    column_basis = column_table(jnp.arange(H, dtype=jnp.int32))
    own_basis = column_table(device * row_count + jnp.arange(row_count, dtype=jnp.int32))
    mode_gain = mode_weights(device * mode_block, mode_block)[:, None, None, None]

    def to_modes(field_data):
        row_modes = row_analysis(field_data, row_basis)
        return lax.psum_scatter(
            column_modes(row_modes, own_basis), "space", scatter_dimension=0, tiled=True
        )

    def to_rows(mode_data):
        column_part = column_synth(mode_data, column_basis)
        return row_synth(
            lax.all_to_all(column_part, "space", split_axis=4, concat_axis=0, tiled=True), row_basis
        )

    input_modes = to_modes(inputs)
    mixed_modes = mix_modes(input_modes, spectral_weight) * mode_gain
    local_term = jnp.einsum(
        "co,schw->sohw", local_weight, inputs, preferred_element_type=jnp.float32
    )
    preact = to_rows(mixed_modes) + local_term + bias_term[None, :, None, None]
    activated, derivative = gelu_parts(preact)
    delta_pre = ((activated - target.astype(jnp.float32)) * derivative).astype(jnp.bfloat16)
    delta_modes = to_modes(delta_pre) * mode_gain
    grad_spectral = mix_grad(input_modes, delta_modes)
    back_modes = mix_back(delta_modes, spectral_weight)
    back_local = jnp.einsum(
        "co,sohw->schw", local_weight, delta_pre, preferred_element_type=jnp.float32
    )
    grad_input = (to_rows(back_modes) + back_local).astype(jnp.bfloat16)
    weight_term = jnp.einsum("schw,sohw->co", inputs, delta_pre, preferred_element_type=jnp.float32)
    bias_sum = jnp.sum(delta_pre, axis=(0, 2, 3), dtype=jnp.float32)
    weight_total, bias_total = lax.psum((weight_term, bias_sum), "space")
    cell_count = inputs.shape[0] * H * W
    return (grad_input, grad_spectral, weight_total / cell_count, bias_total / cell_count)


def solution(mesh):
    return jax.shard_map(
        per_device,
        mesh=mesh,
        in_specs=(
            P("dom", None, "space", None),
            P("dom", None, "space", None),
            P("space", None, None, None),
            P(),
            P(),
        ),
        out_specs=(
            P("dom", None, "space", None),
            P("space", "dom", None, None),
            P("dom", None),
            P("dom"),
        ),
        check_vma=False,
    )
```

profile of v0, /device:TPU:0, one launch (start us, length us, event | category | flops | bytes accessed | tf_op | source)
XLA Modules:
  0.0 490.5 jit_solution(4571138129678116677)
XLA Ops:
  7.2 2.2 multiply_convert_fusion
  9.4 0.3 fusion.101
  9.8 10.8 %fusion.37 = f32[64,2,32,128]{3,0,2,1:T(8,128)} fusion(bf16[1,32,128,2048]{3,2,1,0:T(8,128)(2,1)} %param.5, bf16[1,64,2048]{2,1,0:T(8,128)(2,1)S(1)} %get-tuple-element.42, bf16[1,64,2048]{2,1,0:T(8,128)(2,1)S(1)} %get-tuple-element.43), kind=kOutput, calls=%fused_computation.52 | convolution fusion | flops 2148532224 | bytes 19398656 | tf_op jit(solution)/shard_map/schw,pkw->kpsch/dot_general | solution.py:38
  20.6 4.9 fusion.31
  25.5 0.3 fusion.50
  25.8 0.3 fusion.52
  26.2 1.3 pad_maximum_fusion.1
  27.5 60.3 %reduce-scatter.3.cloned.1.call-done = f32[4,1,32,128]{3,2,0,1:T(8,128)} async-done(((f32[64,1,32,128]{3,2,0,1:T(8,128)}), f32[4,1,32,128]{3,2,0,1:T(8,128)}) %reduce-scatter.3.cloned.1.call-update) | async-done | bytes 65552 | tf_op jit(solution)/shard_map/reduce_scatter | solution.py:127
  87.8 1.0 slice_bitcast_fusion.7
  88.8 1.0 multiply_reduce_fusion.6
  89.9 0.1 maximum_multiply_fusion
  90.0 2.9 fusion.62
  92.9 2.9 fusion.69
  95.8 3.6 fusion.25
  99.4 3.2 fusion.26
  102.7 1.1 pad_maximum_fusion.2
  103.7 6.8 %copy.27 = bf16[4,2,1,32,2048]{3,0,2,1,4:T(4,128)(2,1)} copy(bf16[4,2,1,32,2048]{4,3,0,2,1:T(8,128)(2,1)} %pad_maximum_fusion.2) | data formatting | bytes 2097152 | tf_op jit(solution)/shard_map/stack | solution.py:63
  110.5 7.7 %reshape.437 = bf16[16,2,16384]{2,1,0:T(2,128)(2,1)} reshape(bf16[2048,2,1,4,32]{4,3,2,1,0:T(4,128)(2,1)} %bitcast.233) | data formatting | bytes 2097152
  118.2 4.3 all-to-all-start
  122.6 22.5 %fusion.17 = f32[128,2048,32]{1,2,0:T(8,128)} fusion(bf16[32,128,2048]{2,1,0:T(8,128)(2,1)} %bitcast.229, bf16[32,32]{1,0:T(8,128)(2,1)S(1)} %copy-done), kind=kOutput, calls=%fused_computation.21 | convolution fusion | flops 536870912 | bytes 50333696 | tf_op jit(solution)/shard_map/co,schw->sohw/dot_general | solution.py:139
  145.1 0.3 all-to-all-done
  145.5 7.3 %reshape.438 = bf16[2048,2,1,4,32]{4,3,2,1,0:T(4,128)(2,1)} reshape(bf16[16,2,16384]{2,1,0:T(2,128)(2,1)} %all-to-all-done) | data formatting | bytes 2097152
  152.8 7.1 %copy.28 = bf16[4,2,1,32,16,128]{5,0,4,1,3,2:T(4,128)(2,1)} copy(bf16[4,2,1,32,16,128]{3,0,1,5,4,2:T(4,128)(2,1)} %bitcast.234) | data formatting | bytes 2097152 | tf_op jit(solution)/shard_map/all_to_all | solution.py:134
  159.9 38.7 %convert_reduce_fusion = (f32[32]{0:T(128)S(1)}, bf16[1,32,128,2048]{3,2,1,0:T(8,128)(2,1)}) fusion(bf16[1,32,128,2048]{3,2,1,0:T(8,128)(2,1)} %param.6, f32[32]{0:T(128)S(1)} %copy-done.3, f32[128,2048,32]{1,2,0:T(8,128)} %fusion.17, bf16[64,2,32,128]{3,0,1,2:T(8,128)(2,1)} %bitcast.238, bf16[1,64,2048]{2,1,0:T(8,128)(2,1)S(1)} %get-tuple-element.42, ...), kind=kOutput, calls=%fused_computation.11 | convolution fusion | flops 2290352128 | bytes 68681984 | tf_op jit(solution)/shard_map/kpsch,pkw->schw/dot_general | solution.py:42
  198.6 10.5 %fusion.40 = f32[64,2,32,128]{3,0,2,1:T(8,128)} fusion(bf16[1,32,128,2048]{3,2,1,0:T(8,128)(2,1)} %get-tuple-element.41, bf16[1,64,2048]{2,1,0:T(8,128)(2,1)S(1)} %get-tuple-element.42, bf16[1,64,2048]{2,1,0:T(8,128)(2,1)S(1)} %get-tuple-element.43), kind=kOutput, calls=%fused_computation.53 | convolution fusion | flops 2148532224 | bytes 19398656 | tf_op jit(solution)/shard_map/schw,pkw->kpsch/dot_general | solution.py:38
  209.1 4.6 fusion.34
  213.7 0.6 fusion.49
  214.3 1.3 pad_maximum_fusion.3
  215.7 84.2 %fusion.43 = f32[32,32]{0,1:T(8,128)S(1)} fusion(bf16[32,128,2048]{2,1,0:T(8,128)(2,1)} %bitcast.230, bf16[32,128,2048]{2,1,0:T(8,128)(2,1)} %bitcast.231), kind=kOutput, calls=%fused_computation.54 | convolution fusion | flops 536870912 | bytes 33558528 | tf_op jit(solution)/shard_map/schw,sohw->co/dot_general | solution.py:152
  299.9 62.8 %all-reduce = (f32[32,32]{0,1:T(8,128)S(1)}, f32[32]{0:T(128)S(1)}) all-reduce(f32[32,32]{0,1:T(8,128)S(1)} %fusion.43, f32[32]{0:T(128)S(1)} %get-tuple-element.40), channel_id=1, replica_groups=mesh['dom'=2,'space'=16] {'space'}, use_global_device_ids=true, to_apply=%region_2.3 | all-reduce | flops 1056 | bytes 8448 | tf_op jit(solution)/shard_map/psum | solution.py:154
  362.7 0.9 broadcast_multiply_fusion
  363.6 0.1 slice_bitcast_fusion.2
  363.7 4.3 add_bitcast_fusion
  368.0 2.9 fusion.59
  370.9 2.9 fusion.66
  373.8 3.2 fusion.23
  377.0 3.2 fusion.24
  380.3 0.1 pad_maximum_fusion.4
  380.4 5.0 %copy.34 = bf16[4,2,1,32,2048]{3,0,2,1,4:T(4,128)(2,1)} copy(bf16[4,2,1,32,2048]{4,3,0,2,1:T(8,128)(2,1)S(1)} %pad_maximum_fusion.4) | data formatting | bytes 2097152 | tf_op jit(solution)/shard_map/stack | solution.py:63
  385.4 7.6 %reshape.439 = bf16[16,2,16384]{2,1,0:T(2,128)(2,1)} reshape(bf16[2048,2,1,4,32]{4,3,2,1,0:T(4,128)(2,1)} %bitcast.235) | data formatting | bytes 2097152
  393.0 4.3 all-to-all-start.1
  397.4 0.7 copy.40
  398.0 0.5 broadcast_multiply_fusion.2
  398.6 35.7 %fusion.14 = f32[128,2048,32]{1,2,0:T(8,128)} fusion(bf16[32,128,2048]{2,1,0:T(8,128)(2,1)} %bitcast.232, bf16[32,32]{1,0:T(8,128)(2,1)S(1)} %copy-done), kind=kOutput, calls=%fused_computation.18 | convolution fusion | flops 536870912 | bytes 50333696 | tf_op jit(solution)/shard_map/co,sohw->schw/dot_general | solution.py:148
  434.2 3.6 pad_maximum_fusion
  437.8 7.3 %reshape.440 = bf16[2048,2,1,4,32]{4,3,2,1,0:T(4,128)(2,1)} reshape(bf16[16,2,16384]{2,1,0:T(2,128)(2,1)} %all-to-all-done.1) | data formatting | bytes 2097152
  445.2 6.1 %copy.35 = bf16[4,2,1,32,16,128]{5,0,4,1,3,2:T(4,128)(2,1)S(1)} copy(bf16[4,2,1,32,16,128]{3,0,1,5,4,2:T(4,128)(2,1)} %bitcast.236) | data formatting | bytes 2097152 | tf_op jit(solution)/shard_map/all_to_all | solution.py:134
  451.3 31.9 %fusion.6 = bf16[1,32,128,2048]{3,2,1,0:T(8,128)(2,1)} fusion(f32[128,2048,32]{1,2,0:T(8,128)} %fusion.14, bf16[64,2,32,128]{3,0,1,2:T(8,128)(2,1)S(1)} %bitcast.237, bf16[1,64,2048]{2,1,0:T(8,128)(2,1)S(1)} %get-tuple-element.42, bf16[1,64,2048]{2,1,0:T(8,128)(2,1)S(1)} %get-tuple-element.43), kind=kOutput, calls=%fused_computation.8 | convolution fusion | flops 2164523008 | bytes 51904512 | tf_op jit(solution)/shard_map/kpsch,pkw->schw/dot_general | solution.py:42
  (20 shorter events, 0.2 us)
Async XLA Ops:
  7.2 115.4 %copy-start = (bf16[32,32]{1,0:T(8,128)(2,1)S(1)}, bf16[32,32]{1,0:T(8,128)(2,1)}, u32[]{:S(2)}) copy-start(bf16[32,32]{1,0:T(8,128)(2,1)} %param.8) | copy-start | bytes 6148
  7.2 80.6 %reduce-scatter.3.cloned.1.call-start = ((), (), s32[]{:S(2)}) async-start(), calls=%async_computation.4 | async-start | bytes 1114112 | tf_op jit(solution)/shard_map/reduce_scatter | solution.py:127
  9.8 79.0 %copy-start.1 = (f32[4,32,32,128]{3,2,1,0:T(8,128)S(1)}, f32[4,32,32,128]{3,2,1,0:T(8,128)}, u32[]{:S(2)}) copy-start(f32[4,32,32,128]{3,2,1,0:T(8,128)} %param.7) | copy-start | bytes 6291460
  118.2 27.3 %all-to-all-start = ((bf16[16,2,16384]{2,1,0:T(2,128)(2,1)}), bf16[16,2,16384]{2,1,0:T(2,128)(2,1)}, u32[]{:S(2)}, u32[]{:S(2)}) async-start(bf16[16,2,16384]{2,1,0:T(2,128)(2,1)} %reshape.437), calls=%async_computation.1 | async-start | bytes 2097152 | tf_op jit(solution)/shard_map/all_to_all | solution.py:134
  122.5 240.1 %reduce-scatter.5.cloned.1.call-start = ((), (), s32[]{:S(2)}) async-start(), calls=%async_computation.5 | async-start | bytes 1114112 | tf_op jit(solution)/shard_map/reduce_scatter | solution.py:127
  122.6 37.3 %copy-start.3 = (f32[32]{0:T(128)S(1)}, f32[32]{0:T(128)}, u32[]{:S(2)}) copy-start(f32[32]{0:T(128)} %param.9) | copy-start | bytes 388
  393.0 44.8 %all-to-all-start.1 = ((bf16[16,2,16384]{2,1,0:T(2,128)(2,1)}), bf16[16,2,16384]{2,1,0:T(2,128)(2,1)}, u32[]{:S(2)}, u32[]{:S(2)}) async-start(bf16[16,2,16384]{2,1,0:T(2,128)(2,1)} %reshape.439), calls=%async_computation.3 | async-start | bytes 2097152 | tf_op jit(solution)/shard_map/all_to_all | solution.py:134
  398.6 35.7 %copy-start.2 = (f32[4,32,32,64]{3,2,1,0:T(8,128)S(1)}, f32[4,32,32,64]{3,2,1,0:T(8,128)}, u32[]{:S(2)}) copy-start(f32[4,32,32,64]{3,2,1,0:T(8,128)} %get-tuple-element.28) | copy-start | bytes 3145732
Sparse Core Ops, SparseCore 0:
  27.6 60.1 reduce-scatter.2
  215.8 59.5 reduce-scatter.4
where the time goes:
time: 495 us; the launch traced here: 490 us
  matrix products  269 us (54%)
  blocking collectives  62.8 us (13%)
  waiting for transfers between devices  60.6 us (12%)
  local copies, waits for them, and re-layouts  56.8 us (11%)
  other arithmetic  18 us (4%)
  between operations  14.8 us (3%)
  starting transfers between devices  8.74 us (2%)
    dot_general x1, matrix products, per_device(): jnp.einsum('schw,sohw->co', inputs, delta_pre, preferred_element_type=jnp...  84.2 us
    dot_general x2, matrix products, row_synth(): jnp.einsum('kpsch,pkw->schw', spectra, basis, preferred_element_type=jnp....  70.6 us
    psum x1, blocking collectives, per_device(): weight_total, bias_total = lax.psum((weight_term, bias_sum), 'space')  62.8 us
    reduce_scatter x2, waiting for transfers between devices, to_modes(): lax.psum_scatter(column_modes(row_modes, own_basis), 'space', scatter_dim...  60.3 us
    dot_general x1, matrix products, per_device(): jnp.einsum('co,sohw->schw', local_weight, delta_pre, preferred_element_ty...  35.7 us
    unnamed x15, local copies, waits for them, and re-layouts  31.8 us
    dot_general x1, matrix products, per_device(): jnp.einsum('co,schw->sohw', local_weight, inputs, preferred_element_type=...  22.5 us
    dot_general x2, matrix products, row_analysis(): jnp.einsum('schw,pkw->kpsch', field_data, basis, preferred_element_type=j...  21.3 us
  transfers between devices with their start and end apart: 4, of which 2 were waited for; matrix products, arithmetic and copies ran while one was open for 30% of the time, Pallas kernels for 0%

commit v1 on v0

v1 whole, which is shorter than its diff:
```python
import functools
import math

import jax
import jax.numpy as jnp
import ml_dtypes
import numpy as np
from jax import lax
from jax.experimental import pallas as pl
from jax.experimental.pallas import tpu as pltpu
from jax.sharding import PartitionSpec as P

KX = 64
KY = 64
LANES = 2 * KX
GROUP = 8
F32 = jnp.float32
BF16 = jnp.bfloat16

dot = functools.partial(jnp.dot, preferred_element_type=F32)


def dot_last(a, b):
    return lax.dot_general(a, b, (((1,), (1,)), ((), ())), preferred_element_type=F32)


def params(mib=48):
    return pltpu.CompilerParams(vmem_limit_bytes=mib * 2**20)


def row_basis_table(height, width):
    angles = 2.0 * np.pi / width * (np.arange(KY)[:, None] * np.arange(width)[None, :] % width)
    factor = 1.0 / math.sqrt(height * width)
    table = np.concatenate([np.cos(angles) * factor, -np.sin(angles) * factor])
    return table.astype(np.float32).astype(ml_dtypes.bfloat16)


def column_tables(height):
    index = np.arange(KX)
    frequency = np.where(index < KX // 2, index, index + height - KX)
    angles = 2.0 * np.pi / height * (np.arange(height)[:, None] * frequency[None, :] % height)
    cosines, sines = np.cos(angles), np.sin(angles)

    def parts(table):
        high = table.astype(np.float32).astype(ml_dtypes.bfloat16)
        low = (table - high.astype(np.float64)).astype(np.float32).astype(ml_dtypes.bfloat16)
        return high, low

    synthesis = parts(np.concatenate([cosines, sines], axis=1))
    analysis = parts(np.concatenate([cosines, -sines, sines, cosines], axis=1))
    return np.concatenate(synthesis + analysis, axis=1)


def swap_halves(value):
    return pltpu.roll(value, LANES // 2, 1)


def real_lanes(shape):
    return lax.broadcasted_iota(jnp.int32, shape, 1) < LANES // 2


def column_analysis(row_modes, tables_ref):
    rows = row_modes[0].shape[0]
    first, second = LANES * 2, LANES * 3
    high = [tables_ref[:, first : first + LANES], tables_ref[:, second : second + LANES]]
    low = [tables_ref[:, first + 2 * LANES : first + 3 * LANES], tables_ref[:, second + 2 * LANES : second + 3 * LANES]]
    flipped = [value.T for value in row_modes]
    parts = [[value[:KY] for value in flipped], [value[KY:] for value in flipped]]
    parts = [jnp.concatenate(part, axis=0) for part in parts]
    if rows % 128 == 0:
        parts = [jnp.concatenate(parts, axis=1)]
        high = [jnp.concatenate(high, axis=0)]
        low = [jnp.concatenate(low, axis=0)]
    total = 0.0
    for part, table_high, table_low in zip(parts, high, low):
        part_high = part.astype(BF16)
        part_low = (part - part_high.astype(F32)).astype(BF16)
        total += dot(part_high, table_high) + dot(part_low, table_high) + dot(part_high, table_low)
    return [total[i * KY : (i + 1) * KY] for i in range(len(row_modes))]


def column_synthesis(modes_ref, channel, channels, tables_ref):
    modes = modes_ref[pl.ds(channel, KY, stride=channels), :]
    real = real_lanes(modes.shape)
    both = jnp.concatenate([jnp.where(real, modes, -modes), swap_halves(modes)], axis=0).astype(BF16)
    both = jnp.concatenate([both, both], axis=1)
    return dot_last(tables_ref[:, : 2 * LANES], both).astype(BF16)


def gelu_parts(value):
    normal_cdf = 0.5 * (1.0 + lax.erf(value * (1.0 / math.sqrt(2.0))))
    density = jnp.exp(-0.5 * value * value) * (1.0 / math.sqrt(2.0 * math.pi))
    return (value * normal_cdf, normal_cdf + value * density)


def emit_halves(modes, send_ref, keep_ref):
    half = modes.shape[0] // 2
    keep_ref[...] = modes[:half]
    send_ref[...] = modes[half:].astype(BF16)


def analysis_kernel(block, channels, field_ref, basis_ref, tables_ref, send_ref, keep_ref, modes):
    step = pl.program_id(0)
    rows, width = field_ref.shape[1:]
    product = dot(field_ref[...].reshape(block * rows, width), basis_ref[...])
    parts = column_analysis([product[i * rows : (i + 1) * rows] for i in range(block)], tables_ref)
    for i, part in enumerate(parts):
        modes[pl.ds(step * block + i, KY, stride=channels), :] = part

    @pl.when(step == pl.num_programs(0) - 1)
    def _():
        emit_halves(modes, send_ref, keep_ref)


def half_outputs(channels):
    half = KY // 2 * channels
    specs = [pl.BlockSpec((half, LANES), lambda *_: (0, 0))] * 2
    shapes = [jax.ShapeDtypeStruct((half, LANES), BF16), jax.ShapeDtypeStruct((half, LANES), F32)]
    return specs, shapes


def analyse(field, basis_t, tables, block=4):
    channels, rows, width = field.shape
    specs, shapes = half_outputs(channels)
    return pl.pallas_call(
        functools.partial(analysis_kernel, block, channels),
        grid=(channels // block,),
        in_specs=[
            pl.BlockSpec((block, rows, width), lambda i: (i, 0, 0)),
            pl.BlockSpec(basis_t.shape, lambda i: (0, 0)),
            pl.BlockSpec(tables.shape, lambda i: (0, 0)),
        ],
        out_specs=specs,
        out_shape=shapes,
        scratch_shapes=[pltpu.VMEM((KY * channels, LANES), F32)],
        compiler_params=params(),
        name="analyse",
    )(field, basis_t, tables)


def group_rows(value, start):
    channels, _, width = value.shape
    return value[:, start : start + GROUP, :].reshape(channels * GROUP, width).astype(BF16)


def local_kernel(chunk, field_ref, weight_ref, bias_ref, _, out_ref):
    channels, rows, width = field_ref.shape
    for start in range(0, width, chunk):
        columns = pl.ds(start, chunk)
        field = field_ref[:, :, columns].astype(F32)
        parts = []
        for row in range(0, rows, GROUP):
            part = dot(weight_ref[...], group_rows(field, row)) + bias_ref[...]
            parts.append(part.reshape(channels, GROUP, chunk))
        out_ref[:, :, columns] = jnp.concatenate(parts, axis=1).astype(BF16)


def mix_local(field, weight, bias, out, first, count, block=16, chunk=512):
    channels, rows, width = field.shape
    offset = first // block
    spec = pl.BlockSpec((channels, block, width), lambda i: (0, offset + i, 0))
    whole = lambda array: pl.BlockSpec(array.shape, lambda i: (0, 0))
    return pl.pallas_call(
        functools.partial(local_kernel, chunk),
        grid=(count // block,),
        in_specs=[spec, whole(weight), whole(bias), pl.BlockSpec(memory_space=pl.ANY)],
        out_specs=spec,
        out_shape=jax.ShapeDtypeStruct(field.shape, BF16),
        input_output_aliases={3: 0},
        compiler_params=params(),
        name="mix_local",
    )(field, weight, bias, out)


def back_kernel(chunk, field_ref, delta_ref, weight_ref, _, out_ref, grad_ref):
    channels, rows, width = field_ref.shape
    grad = jnp.zeros(grad_ref.shape, F32)
    for start in range(0, width, chunk):
        columns = pl.ds(start, chunk)
        field = field_ref[:, :, columns].astype(F32)
        delta = delta_ref[:, :, columns].astype(F32)
        parts = []
        for row in range(0, rows, GROUP):
            delta_group = group_rows(delta, row)
            grad += dot_last(group_rows(field, row), delta_group)
            parts.append(dot(weight_ref[...], delta_group).reshape(channels, GROUP, chunk))
        out_ref[:, :, columns] = jnp.concatenate(parts, axis=1).astype(BF16)

    @pl.when(pl.program_id(0) == 0)
    def _():
        grad_ref[...] = grad

    @pl.when(pl.program_id(0) > 0)
    def _():
        grad_ref[...] += grad


def mix_back_local(field, delta, weight, out, first, count, block=16, chunk=512):
    channels, rows, width = field.shape
    offset = first // block
    spec = pl.BlockSpec((channels, block, width), lambda i: (0, offset + i, 0))
    whole = pl.BlockSpec(weight.shape, lambda i: (0, 0))
    return pl.pallas_call(
        functools.partial(back_kernel, chunk),
        grid=(count // block,),
        in_specs=[spec, spec, whole, pl.BlockSpec(memory_space=pl.ANY)],
        out_specs=[spec, whole],
        out_shape=[jax.ShapeDtypeStruct(field.shape, BF16), jax.ShapeDtypeStruct(weight.shape, F32)],
        input_output_aliases={3: 0},
        compiler_params=params(),
        name="mix_back_local",
    )(field, delta, weight, out)


def load_modes(modes, first_ref, second_ref):
    half = first_ref.shape[0]
    modes[:half] = first_ref[...].astype(F32)
    modes[half:] = second_ref[...].astype(F32)


def delta_kernel(
    block, channels, chunk, local_ref, target_ref, first_ref, second_ref, basis_ref, basis_t_ref, tables_ref,
    delta_ref, send_ref, keep_ref, sums_ref, mixed, modes,
):
    step = pl.program_id(0)
    rows, width = local_ref.shape[1:]

    @pl.when(step == 0)
    def _():
        load_modes(mixed, first_ref, second_ref)

    spectra = jnp.concatenate(
        [column_synthesis(mixed, step * block + i, channels, tables_ref) for i in range(block)], axis=0
    )
    product = jnp.zeros((block * rows, LANES), F32)
    for start in range(0, width, chunk):
        columns = pl.ds(start, chunk)
        local = local_ref[:, :, columns].reshape(block * rows, chunk).astype(F32)
        target = target_ref[:, :, columns].reshape(block * rows, chunk).astype(F32)
        activated, derivative = gelu_parts(dot(spectra, basis_ref[:, columns]) + local)
        delta = ((activated - target) * derivative).astype(BF16)
        delta_ref[:, :, columns] = delta.reshape(block, rows, chunk)
        product += dot(delta, basis_t_ref[columns, :])
    row_modes = [product[i * rows : (i + 1) * rows] for i in range(block)]
    for i, part in enumerate(column_analysis(row_modes, tables_ref)):
        modes[pl.ds(step * block + i, KY, stride=channels), :] = part
        sums_ref[pl.ds(step * block + i, 1), :] = jnp.sum(row_modes[i], axis=0, keepdims=True)

    @pl.when(step == pl.num_programs(0) - 1)
    def _():
        emit_halves(modes, send_ref, keep_ref)


def make_delta(local, target, first, second, basis, basis_t, tables, block=4, chunk=512):
    channels, rows, width = local.shape
    field = pl.BlockSpec((block, rows, width), lambda i: (i, 0, 0))
    whole = lambda array: pl.BlockSpec(array.shape, lambda i: (0, 0))
    specs, shapes = half_outputs(channels)
    scratch = pltpu.VMEM((KY * channels, LANES), F32)
    return pl.pallas_call(
        functools.partial(delta_kernel, block, channels, chunk),
        grid=(channels // block,),
        in_specs=[field, field] + [whole(array) for array in (first, second, basis, basis_t, tables)],
        out_specs=[field] + specs + [pl.BlockSpec((channels, LANES), lambda i: (0, 0))],
        out_shape=[jax.ShapeDtypeStruct(local.shape, BF16)]
        + shapes
        + [jax.ShapeDtypeStruct((channels, LANES), F32)],
        scratch_shapes=[scratch, scratch],
        compiler_params=params(),
        name="make_delta",
    )(local, target, first, second, basis, basis_t, tables)


def synthesis_kernel(
    block, channels, chunk, offset, local_ref, first_ref, second_ref, basis_ref, tables_ref, _, out_ref, modes
):
    step = pl.program_id(0)
    rows, width = local_ref.shape[1:]

    @pl.when(step == 0)
    def _():
        load_modes(modes, first_ref, second_ref)

    spectra = jnp.concatenate(
        [column_synthesis(modes, (offset + step) * block + i, channels, tables_ref) for i in range(block)], axis=0
    )
    for start in range(0, width, chunk):
        columns = pl.ds(start, chunk)
        local = local_ref[:, :, columns].reshape(block * rows, chunk).astype(F32)
        value = dot(spectra, basis_ref[:, columns]) + local
        out_ref[:, :, columns] = value.astype(BF16).reshape(block, rows, chunk)


def synthesise(local, first, second, basis, tables, out, start, count, block=4, chunk=512):
    channels, rows, width = local.shape
    offset = start // block
    field = pl.BlockSpec((block, rows, width), lambda i: (offset + i, 0, 0))
    whole = lambda array: pl.BlockSpec(array.shape, lambda i: (0, 0))
    return pl.pallas_call(
        functools.partial(synthesis_kernel, block, channels, chunk, offset),
        grid=(count // block,),
        in_specs=[field]
        + [whole(array) for array in (first, second, basis, tables)]
        + [pl.BlockSpec(memory_space=pl.ANY)],
        out_specs=field,
        out_shape=jax.ShapeDtypeStruct(local.shape, BF16),
        scratch_shapes=[pltpu.VMEM((KY * channels, LANES), F32)],
        input_output_aliases={5: 0},
        compiler_params=params(),
        name="synthesise",
    )(local, first, second, basis, tables, out)


def sum_parts(refs):
    return functools.reduce(lambda a, b: a + b, [ref[...].astype(F32) for ref in refs])


def mix_modes_kernel(count, channels, *refs):
    parts, (weight_ref, gain_ref, mixed_ref, modes_ref) = refs[:-4], refs[-4:]
    modes_ref[...] = sum_parts(parts)
    real = real_lanes((channels, LANES))
    for q in range(count):
        rows = slice(q * channels, (q + 1) * channels)
        modes = modes_ref[rows]
        other = swap_halves(modes)
        first, second = jnp.where(real, modes, other), jnp.where(real, other, -modes)
        direct = jnp.zeros((channels, LANES), F32)
        crossed = jnp.zeros((channels, LANES), F32)
        for c in range(channels):
            weight = weight_ref[q, c]
            direct += first[c : c + 1] * weight
            crossed += second[c : c + 1] * weight
        mixed_ref[rows] = ((direct + swap_halves(crossed)) * gain_ref[q : q + 1]).astype(BF16)


def mix_modes(parts, weight, gain):
    count, channels = weight.shape[:2]
    return pl.pallas_call(
        functools.partial(mix_modes_kernel, count, channels),
        out_shape=[
            jax.ShapeDtypeStruct((count * channels, LANES), BF16),
            jax.ShapeDtypeStruct((count * channels, LANES), F32),
        ],
        compiler_params=params(),
        name="mix_modes",
    )(*parts, weight, gain)


def mix_back_kernel(count, channels, *refs):
    parts, (weight_ref, gain_ref, back_ref, delta_ref) = refs[:-4], refs[-4:]
    delta_ref[...] = sum_parts(parts)
    real = real_lanes((channels, LANES))
    for q in range(count):
        rows = slice(q * channels, (q + 1) * channels)
        delta = delta_ref[rows] * gain_ref[q : q + 1]
        delta_ref[rows] = delta
        other = swap_halves(delta)
        first, second = jnp.where(real, delta, -other), jnp.where(real, other, delta)
        direct, crossed = [], []
        for c in range(channels):
            weight = weight_ref[q, c]
            direct.append(jnp.sum(first * weight, axis=0, keepdims=True))
            crossed.append(jnp.sum(second * weight, axis=0, keepdims=True))
        direct, crossed = jnp.concatenate(direct, axis=0), jnp.concatenate(crossed, axis=0)
        back_ref[rows] = (direct + swap_halves(crossed)).astype(BF16)


def mix_back(parts, weight, gain):
    count, channels = weight.shape[:2]
    return pl.pallas_call(
        functools.partial(mix_back_kernel, count, channels),
        out_shape=[
            jax.ShapeDtypeStruct((count * channels, LANES), BF16),
            jax.ShapeDtypeStruct((count * channels, LANES), F32),
        ],
        compiler_params=params(),
        name="mix_back",
    )(*parts, weight, gain)


def grad_kernel(channels, modes_ref, delta_ref, grad_ref):
    modes, delta = modes_ref[...], delta_ref[...]
    real = real_lanes(modes.shape)
    other, delta_other = swap_halves(modes), swap_halves(delta)
    first, second = jnp.where(real, modes, other), jnp.where(real, other, -modes)
    for c in range(channels):
        grad_ref[0, c] = first[c : c + 1] * delta + second[c : c + 1] * delta_other


def mode_grad(modes, delta, count, channels):
    spec = pl.BlockSpec((channels, LANES), lambda i: (i, 0))
    return pl.pallas_call(
        functools.partial(grad_kernel, channels),
        grid=(count,),
        in_specs=[spec, spec],
        out_specs=pl.BlockSpec((1, channels, channels, LANES), lambda i: (i, 0, 0, 0)),
        out_shape=jax.ShapeDtypeStruct((count, channels, channels, LANES), F32),
        name="mode_grad",
    )(modes, delta)


def fold_kernel(channels, *refs):
    parts, out_ref = refs[:-1], refs[-1]
    size = channels * GROUP
    total = sum_parts(parts)
    row = lax.broadcasted_iota(jnp.int32, (size, size), 0) % GROUP
    column = lax.broadcasted_iota(jnp.int32, (size, size), 1) % GROUP
    total = jnp.where(row == column, total, 0.0)
    wide = lax.broadcasted_iota(jnp.int32, (channels, size), 1) // GROUP
    pick = (wide == lax.broadcasted_iota(jnp.int32, (channels, size), 0)).astype(F32)
    half = jnp.dot(pick, total, precision=lax.Precision.HIGHEST, preferred_element_type=F32)
    out_ref[...] = lax.dot_general(
        half, pick, (((1,), (1,)), ((), ())), precision=lax.Precision.HIGHEST, preferred_element_type=F32
    )


def fold_groups(parts, channels):
    return pl.pallas_call(
        functools.partial(fold_kernel, channels),
        out_shape=jax.ShapeDtypeStruct((channels, channels), F32),
        name="fold_groups",
    )(*parts)


def blank(shape):
    def kernel(out_ref):
        pass

    return pl.pallas_call(
        kernel,
        out_specs=pl.BlockSpec(memory_space=pl.ANY),
        out_shape=jax.ShapeDtypeStruct(shape, BF16),
        name="blank",
    )()


def per_device(devices, inputs, target, spectral_weight, local_weight, bias_term):
    samples, channels, rows, width = inputs.shape
    assert samples == 1
    field, target = inputs[0], target[0]
    height = rows * devices
    count = spectral_weight.shape[0]
    device = lax.axis_index("space")
    far = devices // 4

    place = np.arange(KY) // count
    offset = place // (2 * far) + 2 * (place // far % 2) + 4 * (place % far)
    order = (device ^ jnp.asarray(offset, jnp.int32)) * count + jnp.asarray(np.arange(KY) % count, jnp.int32)
    source = jnp.concatenate([order, order + KY])
    pick = (jnp.arange(LANES, dtype=jnp.int32)[:, None] == source[None, :]).astype(BF16)
    basis_table = row_basis_table(height, width)
    basis_t = dot(jnp.asarray(basis_table.T.copy()), pick).astype(BF16)
    tables = lax.dynamic_slice_in_dim(jnp.asarray(column_tables(height)), device * rows, rows, 0)
    mode_index = device * count + jnp.arange(count, dtype=jnp.int32)
    gain = jnp.broadcast_to(jnp.where(mode_index == 0, 1.0, 2.0).astype(F32)[:, None], (count, LANES))

    def exchange(value, mask):
        return lax.ppermute(value, "space", [(i, i ^ mask) for i in range(devices)])

    barrier = lax.optimization_barrier

    def beside(sent, received, work, state):
        if work is None:
            return received, state
        sent, state = barrier((sent, state))
        return barrier((received, work(state)))

    def reduce_modes(send, keep, work, state):
        received = exchange(send, 1).astype(F32)
        half = keep.shape[0] // 2
        send = (keep[half:] + received[half:]).astype(BF16)
        keep = keep[:half] + received[:half]
        received, state = beside(send, exchange(send, 2), work[0], state)
        total = keep + received.astype(F32)
        size = total.shape[0] // far
        pieces = [total[i * size : (i + 1) * size].astype(BF16) for i in range(1, far)]
        received, state = beside(pieces, [exchange(p, 4 * (i + 1)) for i, p in enumerate(pieces)], work[1], state)
        return [total[:size]] + received, state

    def gather_modes(own, work, state):
        received, state = beside(own, [exchange(own, 4 * i) for i in range(1, far)], work[0], state)
        part = jnp.concatenate([own] + received, axis=0)
        received, state = beside(part, exchange(part, 2), work[1], state)
        part = jnp.concatenate([part, received], axis=0)
        return part, exchange(part, 1), state

    send, keep = analyse(field, basis_t, tables)
    kron = lambda matrix: jnp.kron(matrix, jnp.eye(GROUP, dtype=BF16))
    forward_weight, back_weight = kron(local_weight.T), kron(local_weight)
    bias = jnp.repeat(bias_term, GROUP)[:, None]
    splits = 4 if rows % 64 == 0 else 1
    step = rows // splits

    def local_work(i):
        if i >= splits:
            return None
        return lambda state: mix_local(field, forward_weight, bias, state, i * step, step)

    local = blank(field.shape)
    parts, local = reduce_modes(send, keep, [local_work(0), local_work(1)], local)
    mixed, modes = mix_modes(parts, spectral_weight, gain)
    first, second, local = gather_modes(mixed, [local_work(2), local_work(3)], local)
    basis = lax.dot_general(pick, jnp.asarray(basis_table), (((0,), (0,)), ((), ())), preferred_element_type=F32)
    basis = basis.astype(BF16)
    delta, send, keep, sums = make_delta(local, target, first, second, basis, basis_t, tables)

    def back_work(i):
        if i >= splits:
            return None

        def work(state):
            out, grads = state
            out, grad = mix_back_local(field, delta, back_weight, out, i * step, step)
            return out, grads + [grad]

        return work

    parts, state = reduce_modes(send, keep, [back_work(0), back_work(1)], (local, []))
    back, delta_modes = mix_back(parts, spectral_weight, gain)
    first, second, state = gather_modes(back, [back_work(2), back_work(3)], state)
    back_local, grads = state
    grad_spectral = mode_grad(modes, delta_modes, count, channels)

    def tree(values):
        while len(values) > 1:
            values = [values[i] + values[i + 1] for i in range(0, len(values), 2)]
        return values[0]

    bias_sum = jnp.sum(jnp.where(source[None, :] == 0, sums, 0.0), axis=1) * math.sqrt(height * width)
    shared = jnp.concatenate([fold_groups(grads, channels), bias_sum[:, None]], axis=1)
    split = channels // 2
    near = [exchange(shared, i) for i in range(1, 4)]
    near, grad_input = beside(
        shared, near, lambda out: synthesise(back_local, first, second, basis, tables, out, 0, split), delta
    )
    shared = tree([shared] + near)
    distant = [exchange(shared, 4 * i) for i in range(1, far)]
    distant, grad_input = beside(
        shared, distant, lambda out: synthesise(back_local, first, second, basis, tables, out, split, channels - split),
        grad_input,
    )
    shared = tree([shared] + distant) / (samples * height * width)
    return (grad_input[None], grad_spectral, shared[:, :channels], shared[:, channels])


def solution(mesh):
    return jax.shard_map(
        functools.partial(per_device, mesh.shape["space"]),
        mesh=mesh,
        in_specs=(
            P("dom", None, "space", None),
            P("dom", None, "space", None),
            P("space", None, None, None),
            P(),
            P(),
        ),
        out_specs=(
            P("dom", None, "space", None),
            P("space", "dom", None, None),
            P("dom", None),
            P("dom"),
        ),
        check_vma=False,
    )
```

time: 495 us -> 165 us (0.33)
  matrix products: 269 us -> 1.68 us
  Pallas kernels: 0 us -> 111 us
  blocking collectives: 62.8 us -> 0 us
  waiting for transfers between devices: 60.6 us -> 3.94 us
  local copies, waits for them, and re-layouts: 56.8 us -> 10.9 us
  starting transfers between devices: 8.74 us -> 30.5 us
  between operations: 14.8 us -> 1.02 us
  other arithmetic: 18 us -> 5.33 us
    dot_general x17 -> x2, matrix products: 269 us -> 1.68 us  [the longest x1 1.33 us: per_device(): basis_t = dot(jnp.asarray(basis_table.T.copy()), pick).astype(BF16)]
    pallas_call x0 -> x17, Pallas kernels: none -> 111 us  [the longest x1 31.7 us: make_delta(): pl.pallas_call(functools.partial(delta_kernel, block, channels, chunk), g...]
    psum x1 -> x0, blocking collectives: 62.8 us -> none  [per_device(): weight_total, bias_total = lax.psum((weight_term, bias_sum), 'space')]
    reduce_scatter x2 -> x0, waiting for transfers between devices: 60.3 us -> none  [to_modes(): lax.psum_scatter(column_modes(row_modes, own_basis), 'space', scatter_dim...]
    unnamed x15 -> x40, local copies, waits for them, and re-layouts: 31.8 us -> 0.66 us
    ppermute x0 -> x26, starting transfers between devices: none -> 30.5 us  [exchange(): return lax.ppermute(value, 'space', [(i, i ^ mask) for i in range(devices)])]
    all_to_all x2 -> x0, local copies, waits for them, and re-layouts: 13.2 us -> none  [to_rows(): lax.all_to_all(column_part, 'space', split_axis=4, concat_axis=0, tiled=T...]
    another operation x2 -> x1, local copies, waits for them, and re-layouts: 11.8 us -> 0.1 us  [per_device(): bias = jnp.repeat(bias_term, GROUP)[:, None]]
  transfers between devices with their start and end apart: 4 -> 26, of which waited for: 2 -> 4; matrix products, arithmetic and copies ran while one was open for 30% -> 7% of each run, Pallas kernels for 0% -> 40%
where the time goes in v1:
time: 165 us; the launch traced here: 164 us
  Pallas kernels  111 us (67%)
  starting transfers between devices  30.5 us (18%)
  local copies, waits for them, and re-layouts  10.9 us (7%)
  other arithmetic  5.33 us (3%)
  waiting for transfers between devices  3.94 us (2%)
  matrix products  1.68 us (1%)
    pallas_call x1, Pallas kernels, make_delta(): pl.pallas_call(functools.partial(delta_kernel, block, channels, chunk), g...  31.7 us
    ppermute x26, starting transfers between devices, exchange(): return lax.ppermute(value, 'space', [(i, i ^ mask) for i in range(devices)])  30.5 us
    pallas_call x4, Pallas kernels, mix_back_local(): pl.pallas_call(functools.partial(back_kernel, chunk), grid=(count // bloc...  24.6 us
    pallas_call x2, Pallas kernels, synthesise(): pl.pallas_call(functools.partial(synthesis_kernel, block, channels, chunk...  17.8 us
    pallas_call x4, Pallas kernels, mix_local(): pl.pallas_call(functools.partial(local_kernel, chunk), grid=(count // blo...  17.5 us
    pallas_call x1, Pallas kernels, analyse(): pl.pallas_call(functools.partial(analysis_kernel, block, channels), grid=...  12.8 us
    mul x2, local copies, waits for them, and re-layouts, per_device(): kron = lambda matrix: jnp.kron(matrix, jnp.eye(GROUP, dtype=BF16))  8.11 us
    ppermute x26, waiting for transfers between devices, exchange(): return lax.ppermute(value, 'space', [(i, i ^ mask) for i in range(devices)])  3.94 us
  transfers between devices with their start and end apart: 26, of which 4 were waited for; matrix products, arithmetic and copies ran while one was open for 7% of the time, Pallas kernels for 40%

profile of v1, /device:TPU:0, one launch (start us, length us, event | category | flops | bytes accessed | tf_op | source)
XLA Modules:
  0.0 164.3 jit_solution(13471807945634130048)
XLA Ops:
  0.6 0.7 multiply_add_fusion
  1.4 0.9 constant_dynamic-slice_fusion.tables_ref
  2.4 1.3 fusion.basis_ref.basis_t_ref
  3.7 12.8 %analyse.1 = (bf16[1024,128]{1,0:T(8,128)(2,1)S(1)}, f32[1024,128]{1,0:T(8,128)S(1)}) custom-call(bf16[32,128,2048]{2,1,0:T(8,128)(2,1)} %bitcast.15, bf16[2048,128]{1,0:T(8,128)(2,1)S(1)} %fusion.basis_ref.basis_t_ref, bf16[128,768]{1,0:T(8,128)(2,1)S(1)} %constant_dynamic-slice_fusion.tables_ref), custom_call_target="tpu_custom_call" | custom-call | tf_op jit(solution)/shard_map/analyse/pallas_call | solution.py:125
  16.6 0.5 collective-permute-start
  17.2 1.1 collective-permute-done
  18.3 3.0 %collective-permute-start.1 = (bf16[512,128]{1,0:T(8,128)(2,1)S(1)}, bf16[512,128]{1,0:T(8,128)(2,1)S(1)}, u32[]{:S(2)}, u32[]{:S(2)}) collective-permute-start(bf16[512,128]{1,0:T(8,128)(2,1)S(1)} %fusion.3), channel_id=1, source_target_pairs={{0,2},{1,3},{2,0},{3,1},{4,6},{5,7},{6,4},{7,5},{8,10},{9,11},{10,... | collective-permute-start | bytes 393224 | tf_op jit(solution)/shard_map/ppermute | solution.py:458
  21.3 2.4 %broadcast_multiply_fusion = (bf16[32,8,32,8]{3,2,1,0:T(8,128)(2,1)}, bf16[32,8,32,8]{3,2,1,0:T(8,128)(2,1)}) fusion(bf16[32,32]{1,0:T(8,128)(2,1)S(1)} %copy-done.14, bf16[8,8]{1,0:T(8,128)(2,1)S(1)} %fusion.7, bf16[32,32]{1,0:T(8,128)(2,1)S(1)} %copy.28), kind=kLoop, calls=%fused_computation.3 | loop fusion | flops 131072 | bytes 266368 | tf_op jit(solution)/shard_map/jit(kron)/mul | solution.py:488
  23.8 4.1 %mul.75.weight_ref = bf16[256,256]{1,0:T(8,128)(2,1)S(1)} reshape(bf16[32,8,32,8]{3,2,1,0:T(8,128)(2,1)} %get-tuple-element.185) | data formatting | bytes 262144 | tf_op jit(solution)/shard_map/jit(kron)/mul | solution.py:488
  27.9 4.3 %mix_local.4._ = bf16[32,128,2048]{2,1,0:T(8,128)(2,1)} custom-call(bf16[32,128,2048]{2,1,0:T(8,128)(2,1)} %bitcast.16, bf16[256,256]{1,0:T(8,128)(2,1)S(1)} %mul.75.weight_ref, f32[256,1]{1,0:T(8,128)S(1)} %broadcast_in_dim_reshape.4.bias_ref, bf16[32,128,2048]{2,1,0:T(8,128)(2,1)} %blank.1._), custom_call_target="tpu_custom_call", output_to_operand_aliasing={{}: (3, {})} | custom-call | tf_op jit(solution)/shard_map/mix_local/pallas_call | solution.py:163
  32.3 3.7 %collective-permute-start.4 = (bf16[128,128]{1,0:T(8,128)(2,1)S(1)}, bf16[128,128]{1,0:T(8,128)(2,1)S(1)}, u32[]{:S(2)}, u32[]{:S(2)}) collective-permute-start(bf16[128,128]{1,0:T(8,128)(2,1)S(1)} %get-tuple-element.165), channel_id=1, source_target_pairs={{0,12},{1,13},{2,14},{3,15},{4,8},{5,9},{6,10},{7,11},{8,4},{9,5},... | collective-permute-start | bytes 98312 | tf_op jit(solution)/shard_map/ppermute | solution.py:458
  35.9 0.8 collective-permute-start.2
  36.7 4.5 %mix_local.5._ = bf16[32,128,2048]{2,1,0:T(8,128)(2,1)} custom-call(bf16[32,128,2048]{2,1,0:T(8,128)(2,1)} %bitcast.17, bf16[256,256]{1,0:T(8,128)(2,1)S(1)} %mul.75.weight_ref, f32[256,1]{1,0:T(8,128)S(1)} %broadcast_in_dim_reshape.4.bias_ref, bf16[32,128,2048]{2,1,0:T(8,128)(2,1)} %mix_local.4._), custom_call_target="tpu_custom_call", output_to_operand_aliasing={{}: (3, {})} | custom-call | tf_op jit(solution)/shard_map/mix_local/pallas_call | solution.py:163
  41.3 0.4 mix_modes.1
  41.8 3.7 %collective-permute-start.7 = (bf16[128,128]{1,0:T(8,128)(2,1)S(1)}, bf16[128,128]{1,0:T(8,128)(2,1)S(1)}, u32[]{:S(2)}, u32[]{:S(2)}) collective-permute-start(bf16[128,128]{1,0:T(8,128)(2,1)S(1)} %get-tuple-element.89), channel_id=1, source_target_pairs={{0,12},{1,13},{2,14},{3,15},{4,8},{5,9},{6,10},{7,11},{8,4},{9,5},... | collective-permute-start | bytes 98312 | tf_op jit(solution)/shard_map/ppermute | solution.py:458
  45.4 0.8 collective-permute-start.5
  46.2 4.3 %mix_local.6._ = bf16[32,128,2048]{2,1,0:T(8,128)(2,1)} custom-call(bf16[32,128,2048]{2,1,0:T(8,128)(2,1)} %bitcast.18, bf16[256,256]{1,0:T(8,128)(2,1)S(1)} %mul.75.weight_ref, f32[256,1]{1,0:T(8,128)S(1)} %broadcast_in_dim_reshape.4.bias_ref, bf16[32,128,2048]{2,1,0:T(8,128)(2,1)} %mix_local.5._), custom_call_target="tpu_custom_call", output_to_operand_aliasing={{}: (3, {})} | custom-call | tf_op jit(solution)/shard_map/mix_local/pallas_call | solution.py:163
  50.7 0.4 collective-permute-start.8
  51.1 4.4 %mix_local.7.local_ref._ = bf16[32,128,2048]{2,1,0:T(8,128)(2,1)} custom-call(bf16[32,128,2048]{2,1,0:T(8,128)(2,1)} %bitcast.19, bf16[256,256]{1,0:T(8,128)(2,1)S(1)} %mul.75.weight_ref, f32[256,1]{1,0:T(8,128)S(1)} %broadcast_in_dim_reshape.4.bias_ref, bf16[32,128,2048]{2,1,0:T(8,128)(2,1)} %mix_local.6._), custom_call_target="tpu_custom_call", output_to_operand_aliasing={{}: (3, {})} | custom-call | tf_op jit(solution)/shard_map/mix_local/pallas_call | solution.py:163
  55.4 0.3 collective-permute-done.8
  55.8 0.3 convolution_convert_fusion.basis_ref
  56.1 1.2 collective-permute-done.9.second_ref
  57.3 31.7 %make_delta.1 = (bf16[32,128,2048]{2,1,0:T(8,128)(2,1)}, bf16[1024,128]{1,0:T(8,128)(2,1)S(1)}, f32[1024,128]{1,0:T(8,128)S(1)}, f32[32,128]{1,0:T(8,128)S(1)}) custom-call(bf16[32,128,2048]{2,1,0:T(8,128)(2,1)} %mix_local.7.local_ref._, bf16[32,128,2048]{2,1,0:T(8,128)(2,1)} %bitcast.25, ...), custom_call_target="tpu_custom_call" | custom-call | tf_op jit(solution)/shard_map/make_delta/pallas_call | solution.py:260
  89.1 1.4 collective-permute-done.10
  90.6 1.5 collective-permute-start.11
  92.1 4.1 %mul.79.weight_ref = bf16[256,256]{1,0:T(8,128)(2,1)S(1)} reshape(bf16[32,8,32,8]{3,2,1,0:T(8,128)(2,1)} %get-tuple-element.184) | data formatting | bytes 262144 | tf_op jit(solution)/shard_map/jit(kron)/mul | solution.py:488
  96.2 6.2 %mix_back_local.4 = (bf16[32,128,2048]{2,1,0:T(8,128)(2,1)}, f32[256,256]{1,0:T(8,128)S(1)}) custom-call(bf16[32,128,2048]{2,1,0:T(8,128)(2,1)} %bitcast.20, bf16[32,128,2048]{2,1,0:T(8,128)(2,1)} %get-tuple-element.144.delta_ref._, bf16[256,256]{1,0:T(8,128)(2,1)S(1)} %mul.79.weight_ref, ...), custom_call_target="tpu_custom_call", output_to_operand_aliasing={{0}: (3, {})} | custom-call | tf_op jit(solution)/shard_map/mix_back_local/pallas_call | solution.py:203
  102.4 1.0 fusion.8
  103.4 3.7 %collective-permute-start.14 = (bf16[128,128]{1,0:T(8,128)(2,1)S(1)}, bf16[128,128]{1,0:T(8,128)(2,1)S(1)}, u32[]{:S(2)}, u32[]{:S(2)}) collective-permute-start(bf16[128,128]{1,0:T(8,128)(2,1)S(1)} %get-tuple-element.162), channel_id=1, source_target_pairs={{0,12},{1,13},{2,14},{3,15},{4,8},{5,9},{6,10},{7,11},{8,4},{9,5},... | collective-permute-start | bytes 98312 | tf_op jit(solution)/shard_map/ppermute | solution.py:458
  107.1 0.8 collective-permute-start.12
  107.9 6.1 %mix_back_local.5 = (bf16[32,128,2048]{2,1,0:T(8,128)(2,1)}, f32[256,256]{1,0:T(8,128)S(1)}) custom-call(bf16[32,128,2048]{2,1,0:T(8,128)(2,1)} %bitcast.21, bf16[32,128,2048]{2,1,0:T(8,128)(2,1)} %get-tuple-element.144.delta_ref._, bf16[256,256]{1,0:T(8,128)(2,1)S(1)} %mul.79.weight_ref, ...), custom_call_target="tpu_custom_call", output_to_operand_aliasing={{0}: (3, {})} | custom-call | tf_op jit(solution)/shard_map/mix_back_local/pallas_call | solution.py:203
  114.1 0.6 mix_back.1
  114.6 3.7 %collective-permute-start.17 = (bf16[128,128]{1,0:T(8,128)(2,1)S(1)}, bf16[128,128]{1,0:T(8,128)(2,1)S(1)}, u32[]{:S(2)}, u32[]{:S(2)}) collective-permute-start(bf16[128,128]{1,0:T(8,128)(2,1)S(1)} %get-tuple-element.115), channel_id=1, source_target_pairs={{0,12},{1,13},{2,14},{3,15},{4,8},{5,9},{6,10},{7,11},{8,4},{9,5},... | collective-permute-start | bytes 98312 | tf_op jit(solution)/shard_map/ppermute | solution.py:458
  118.3 0.8 collective-permute-start.15
  119.1 6.1 %mix_back_local.6 = (bf16[32,128,2048]{2,1,0:T(8,128)(2,1)}, f32[256,256]{1,0:T(8,128)S(1)}) custom-call(bf16[32,128,2048]{2,1,0:T(8,128)(2,1)} %bitcast.22, bf16[32,128,2048]{2,1,0:T(8,128)(2,1)} %get-tuple-element.144.delta_ref._, bf16[256,256]{1,0:T(8,128)(2,1)S(1)} %mul.79.weight_ref, ...), custom_call_target="tpu_custom_call", output_to_operand_aliasing={{0}: (3, {})} | custom-call | tf_op jit(solution)/shard_map/mix_back_local/pallas_call | solution.py:203
  125.3 0.7 collective-permute-start.18
  126.2 6.1 %mix_back_local.7 = (bf16[32,128,2048]{2,1,0:T(8,128)(2,1)}, f32[256,256]{1,0:T(8,128)S(1)}) custom-call(bf16[32,128,2048]{2,1,0:T(8,128)(2,1)} %bitcast.23, bf16[32,128,2048]{2,1,0:T(8,128)(2,1)} %get-tuple-element.144.delta_ref._, bf16[256,256]{1,0:T(8,128)(2,1)S(1)} %mul.79.weight_ref, ...), custom_call_target="tpu_custom_call", output_to_operand_aliasing={{0}: (3, {})} | custom-call | tf_op jit(solution)/shard_map/mix_back_local/pallas_call | solution.py:203
  132.5 0.5 copy-done.6
  133.0 2.3 %fold_groups.1 = f32[32,32]{1,0:T(8,128)} custom-call(f32[256,256]{1,0:T(8,128)} %copy-done.3, f32[256,256]{1,0:T(8,128)} %copy-done.4, f32[256,256]{1,0:T(8,128)} %copy-done.5, f32[256,256]{1,0:T(8,128)} %copy-done.6), custom_call_target="tpu_custom_call" | custom-call | tf_op jit(solution)/shard_map/fold_groups/pallas_call | solution.py:418
  135.3 0.8 pad_maximum_fusion
  136.1 1.0 collective-permute-start.21
  137.0 0.7 collective-permute-start.20
  137.9 8.9 %synthesise.2._ = bf16[32,128,2048]{2,1,0:T(8,128)(2,1)} custom-call(bf16[32,128,2048]{2,1,0:T(8,128)(2,1)} %get-tuple-element.142.local_ref, bf16[1024,128]{1,0:T(8,128)(2,1)S(1)} %constant_dynamic-update-slice_fusion.13.first_ref, bf16[1024,128]{1,0:T(8,128)(2,1)S(1)} %collective-permute-done.22.second_ref, ...), custom_call_target="tpu_custom_call", output_to_operand_aliasing={{}: (5, {})} | custom-call | tf_op jit(solution)/shard_map/synthesise/pallas_call | solution.py:299
  146.9 3.6 %collective-permute-start.25 = (f32[32,33]{1,0:T(8,128)S(1)}, f32[32,33]{1,0:T(8,128)S(1)}, u32[]{:S(2)}, u32[]{:S(2)}) collective-permute-start(f32[32,33]{1,0:T(8,128)S(1)} %add_add_fusion), channel_id=1, source_target_pairs={{0,12},{1,13},{2,14},{3,15},{4,8},{5,9},{6,10},{7,11},{8,4},{9,5},... | collective-permute-start | bytes 12680 | tf_op jit(solution)/shard_map/ppermute | solution.py:458
  150.5 0.8 collective-permute-start.23
  151.3 3.4 %mode_grad.1 = f32[4,32,32,128]{3,2,1,0:T(8,128)} custom-call(f32[128,128]{1,0:T(8,128)} %copy-done.7, f32[128,128]{1,0:T(8,128)} %copy-done.8), custom_call_target="tpu_custom_call" | custom-call | tf_op jit(solution)/shard_map/mode_grad/pallas_call | solution.py:392
  154.7 8.9 %synthesise.3 = bf16[32,128,2048]{2,1,0:T(8,128)(2,1)} custom-call(bf16[32,128,2048]{2,1,0:T(8,128)(2,1)} %get-tuple-element.142.local_ref, bf16[1024,128]{1,0:T(8,128)(2,1)S(1)} %constant_dynamic-update-slice_fusion.13.first_ref, bf16[1024,128]{1,0:T(8,128)(2,1)S(1)} %collective-permute-done.22.second_ref, ...), custom_call_target="tpu_custom_call", output_to_operand_aliasing={{}: (5, {})} | custom-call | tf_op jit(solution)/shard_map/synthesise/pallas_call | solution.py:299
  163.6 0.7 slice_reduce_fusion
  (94 shorter events, 1.7 us)
Async XLA Ops:
  0.6 16.4 %copy-start.14 = (bf16[32,32]{1,0:T(8,128)(2,1)S(1)}, bf16[32,32]{1,0:T(8,128)(2,1)}, u32[]{:S(2)}) copy-start(bf16[32,32]{1,0:T(8,128)(2,1)} %param.13) | copy-start | bytes 6148
  3.7 19.9 %copy-start.15 = (f32[32]{0:T(128)S(1)}, f32[32]{0:T(128)}, u32[]{:S(2)}) copy-start(f32[32]{0:T(128)} %param.14) | copy-start | bytes 388
  16.6 1.7 %collective-permute-start = (bf16[1024,128]{1,0:T(8,128)(2,1)S(1)}, bf16[1024,128]{1,0:T(8,128)(2,1)S(1)}, u32[]{:S(2)}, u32[]{:S(2)}) collective-permute-start(bf16[1024,128]{1,0:T(8,128)(2,1)S(1)} %get-tuple-element.81), channel_id=1, source_target_pairs={{0,1},{1,0},{2,3},{3,2},{4,5},{5,4},{6,7},{7,6},{8,9},{9,8},{10,11... | collective-permute-start | bytes 786440 | tf_op jit(solution)/shard_map/ppermute | solution.py:458
  18.3 13.9 %collective-permute-start.1 = (bf16[512,128]{1,0:T(8,128)(2,1)S(1)}, bf16[512,128]{1,0:T(8,128)(2,1)S(1)}, u32[]{:S(2)}, u32[]{:S(2)}) collective-permute-start(bf16[512,128]{1,0:T(8,128)(2,1)S(1)} %fusion.3), channel_id=1, source_target_pairs={{0,2},{1,3},{2,0},{3,1},{4,6},{5,7},{6,4},{7,5},{8,10},{9,11},{10,... | collective-permute-start | bytes 393224 | tf_op jit(solution)/shard_map/ppermute | solution.py:458
  32.3 9.0 %collective-permute-start.4 = (bf16[128,128]{1,0:T(8,128)(2,1)S(1)}, bf16[128,128]{1,0:T(8,128)(2,1)S(1)}, u32[]{:S(2)}, u32[]{:S(2)}) collective-permute-start(bf16[128,128]{1,0:T(8,128)(2,1)S(1)} %get-tuple-element.165), channel_id=1, source_target_pairs={{0,12},{1,13},{2,14},{3,15},{4,8},{5,9},{6,10},{7,11},{8,4},{9,5},... | collective-permute-start | bytes 98312 | tf_op jit(solution)/shard_map/ppermute | solution.py:458
  35.9 5.3 %collective-permute-start.3 = (bf16[128,128]{1,0:T(8,128)(2,1)S(1)}, bf16[128,128]{1,0:T(8,128)(2,1)S(1)}, u32[]{:S(2)}, u32[]{:S(2)}) collective-permute-start(bf16[128,128]{1,0:T(8,128)(2,1)S(1)} %get-tuple-element.166), channel_id=1, source_target_pairs={{0,8},{1,9},{2,10},{3,11},{4,12},{5,13},{6,14},{7,15},{8,0},{9,1},... | collective-permute-start | bytes 98312 | tf_op jit(solution)/shard_map/ppermute | solution.py:458
  35.9 5.3 %collective-permute-start.2 = (bf16[128,128]{1,0:T(8,128)(2,1)S(1)}, bf16[128,128]{1,0:T(8,128)(2,1)S(1)}, u32[]{:S(2)}, u32[]{:S(2)}) collective-permute-start(bf16[128,128]{1,0:T(8,128)(2,1)S(1)} %get-tuple-element.167), channel_id=1, source_target_pairs={{0,4},{1,5},{2,6},{3,7},{4,0},{5,1},{6,2},{7,3},{8,12},{9,13},{10,... | collective-permute-start | bytes 98312 | tf_op jit(solution)/shard_map/ppermute | solution.py:458
  36.7 4.6 %copy-start = (f32[4,32,32,128]{3,2,1,0:T(8,128)S(1)}, f32[4,32,32,128]{3,2,1,0:T(8,128)}, u32[]{:S(2)}) copy-start(f32[4,32,32,128]{3,2,1,0:T(8,128)} %refs_4_.3) | copy-start | bytes 6291460
  41.7 8.8 %copy-start.7 = (f32[128,128]{1,0:T(8,128)}, f32[128,128]{1,0:T(8,128)S(1)}, u32[]{:S(2)}) copy-start(f32[128,128]{1,0:T(8,128)S(1)} %get-tuple-element.151.modes_ref) | copy-start | bytes 196612
  41.8 8.8 %collective-permute-start.7 = (bf16[128,128]{1,0:T(8,128)(2,1)S(1)}, bf16[128,128]{1,0:T(8,128)(2,1)S(1)}, u32[]{:S(2)}, u32[]{:S(2)}) collective-permute-start(bf16[128,128]{1,0:T(8,128)(2,1)S(1)} %get-tuple-element.89), channel_id=1, source_target_pairs={{0,12},{1,13},{2,14},{3,15},{4,8},{5,9},{6,10},{7,11},{8,4},{9,5},... | collective-permute-start | bytes 98312 | tf_op jit(solution)/shard_map/ppermute | solution.py:458
  45.4 5.1 %collective-permute-start.6 = (bf16[128,128]{1,0:T(8,128)(2,1)S(1)}, bf16[128,128]{1,0:T(8,128)(2,1)S(1)}, u32[]{:S(2)}, u32[]{:S(2)}) collective-permute-start(bf16[128,128]{1,0:T(8,128)(2,1)S(1)} %get-tuple-element.89), channel_id=1, source_target_pairs={{0,8},{1,9},{2,10},{3,11},{4,12},{5,13},{6,14},{7,15},{8,0},{9,1},... | collective-permute-start | bytes 98312 | tf_op jit(solution)/shard_map/ppermute | solution.py:458
  45.4 5.2 %collective-permute-start.5 = (bf16[128,128]{1,0:T(8,128)(2,1)S(1)}, bf16[128,128]{1,0:T(8,128)(2,1)S(1)}, u32[]{:S(2)}, u32[]{:S(2)}) collective-permute-start(bf16[128,128]{1,0:T(8,128)(2,1)S(1)} %get-tuple-element.89), channel_id=1, source_target_pairs={{0,4},{1,5},{2,6},{3,7},{4,0},{5,1},{6,2},{7,3},{8,12},{9,13},{10,... | collective-permute-start | bytes 98312 | tf_op jit(solution)/shard_map/ppermute | solution.py:458
  50.6 5.1 %copy-start.11 = (bf16[128,2048]{1,0:T(8,128)(2,1)S(1)}, bf16[128,2048]{1,0:T(8,128)(2,1)}, u32[]{:S(2)}) copy-start(bf16[128,2048]{1,0:T(8,128)(2,1)} %constant.42.clone) | copy-start | bytes 1572868
  50.7 5.0 %collective-permute-start.8 = (bf16[512,128]{1,0:T(8,128)(2,1)S(1)}, bf16[512,128]{1,0:T(8,128)(2,1)S(1)}, u32[]{:S(2)}, u32[]{:S(2)}) collective-permute-start(bf16[512,128]{1,0:T(8,128)(2,1)S(1)} %get-tuple-element.177), channel_id=1, source_target_pairs={{0,2},{1,3},{2,0},{3,1},{4,6},{5,7},{6,4},{7,5},{8,10},{9,11},{10,... | collective-permute-start | bytes 393224 | tf_op jit(solution)/shard_map/ppermute | solution.py:458
  55.7 1.6 collective-permute-start.9
  89.0 3.1 %copy-start.1 = (f32[1024,128]{1,0:T(8,128)}, f32[1024,128]{1,0:T(8,128)S(1)}, u32[]{:S(2)}) copy-start(f32[1024,128]{1,0:T(8,128)S(1)} %get-tuple-element.99) | copy-start | bytes 1572868
  89.0 1.5 collective-permute-start.10
  90.5 1.5 copy-start.9
  90.6 11.8 %collective-permute-start.11 = (bf16[512,128]{1,0:T(8,128)(2,1)S(1)}, bf16[512,128]{1,0:T(8,128)(2,1)}, u32[]{:S(2)}, u32[]{:S(2)}) collective-permute-start(bf16[512,128]{1,0:T(8,128)(2,1)S(1)} %fusion.1), channel_id=1, source_target_pairs={{0,2},{1,3},{2,0},{3,1},{4,6},{5,7},{6,4},{7,5},{8,10},{9,11},{10,... | collective-permute-start | bytes 393224 | tf_op jit(solution)/shard_map/ppermute | solution.py:458
  96.1 6.2 %copy-start.2 = (f32[1024,128]{1,0:T(8,128)S(1)}, f32[1024,128]{1,0:T(8,128)}, u32[]{:S(2)}) copy-start(f32[1024,128]{1,0:T(8,128)} %copy-done.1) | copy-start | bytes 1572868
  96.2 6.2 %copy-start.10 = (f32[1024,128]{1,0:T(8,128)S(1)}, f32[1024,128]{1,0:T(8,128)}, u32[]{:S(2)}) copy-start(f32[1024,128]{1,0:T(8,128)} %copy-done.9) | copy-start | bytes 1572868
  102.4 5.5 %copy-start.3 = (f32[256,256]{1,0:T(8,128)}, f32[256,256]{1,0:T(8,128)S(1)}, u32[]{:S(2)}) copy-start(f32[256,256]{1,0:T(8,128)S(1)} %get-tuple-element.137.refs_0_) | copy-start | bytes 786436
  103.4 10.6 %collective-permute-start.14 = (bf16[128,128]{1,0:T(8,128)(2,1)S(1)}, bf16[128,128]{1,0:T(8,128)(2,1)S(1)}, u32[]{:S(2)}, u32[]{:S(2)}) collective-permute-start(bf16[128,128]{1,0:T(8,128)(2,1)S(1)} %get-tuple-element.162), channel_id=1, source_target_pairs={{0,12},{1,13},{2,14},{3,15},{4,8},{5,9},{6,10},{7,11},{8,4},{9,5},... | collective-permute-start | bytes 98312 | tf_op jit(solution)/shard_map/ppermute | solution.py:458
  107.1 6.9 %collective-permute-start.13 = (bf16[128,128]{1,0:T(8,128)(2,1)S(1)}, bf16[128,128]{1,0:T(8,128)(2,1)S(1)}, u32[]{:S(2)}, u32[]{:S(2)}) collective-permute-start(bf16[128,128]{1,0:T(8,128)(2,1)S(1)} %get-tuple-element.163), channel_id=1, source_target_pairs={{0,8},{1,9},{2,10},{3,11},{4,12},{5,13},{6,14},{7,15},{8,0},{9,1},... | collective-permute-start | bytes 98312 | tf_op jit(solution)/shard_map/ppermute | solution.py:458
  107.1 6.9 %collective-permute-start.12 = (bf16[128,128]{1,0:T(8,128)(2,1)S(1)}, bf16[128,128]{1,0:T(8,128)(2,1)S(1)}, u32[]{:S(2)}, u32[]{:S(2)}) collective-permute-start(bf16[128,128]{1,0:T(8,128)(2,1)S(1)} %get-tuple-element.164), channel_id=1, source_target_pairs={{0,4},{1,5},{2,6},{3,7},{4,0},{5,1},{6,2},{7,3},{8,12},{9,13},{10,... | collective-permute-start | bytes 98312 | tf_op jit(solution)/shard_map/ppermute | solution.py:458
  114.0 4.3 %copy-start.4 = (f32[256,256]{1,0:T(8,128)}, f32[256,256]{1,0:T(8,128)S(1)}, u32[]{:S(2)}) copy-start(f32[256,256]{1,0:T(8,128)S(1)} %get-tuple-element.138.refs_1_) | copy-start | bytes 786436
  114.6 10.6 %copy-start.8 = (f32[128,128]{1,0:T(8,128)}, f32[128,128]{1,0:T(8,128)S(1)}, u32[]{:S(2)}) copy-start(f32[128,128]{1,0:T(8,128)S(1)} %get-tuple-element.152.delta_ref) | copy-start | bytes 196612
  114.6 10.6 %collective-permute-start.17 = (bf16[128,128]{1,0:T(8,128)(2,1)S(1)}, bf16[128,128]{1,0:T(8,128)(2,1)S(1)}, u32[]{:S(2)}, u32[]{:S(2)}) collective-permute-start(bf16[128,128]{1,0:T(8,128)(2,1)S(1)} %get-tuple-element.115), channel_id=1, source_target_pairs={{0,12},{1,13},{2,14},{3,15},{4,8},{5,9},{6,10},{7,11},{8,4},{9,5},... | collective-permute-start | bytes 98312 | tf_op jit(solution)/shard_map/ppermute | solution.py:458
  118.3 6.9 %collective-permute-start.16 = (bf16[128,128]{1,0:T(8,128)(2,1)S(1)}, bf16[128,128]{1,0:T(8,128)(2,1)S(1)}, u32[]{:S(2)}, u32[]{:S(2)}) collective-permute-start(bf16[128,128]{1,0:T(8,128)(2,1)S(1)} %get-tuple-element.115), channel_id=1, source_target_pairs={{0,8},{1,9},{2,10},{3,11},{4,12},{5,13},{6,14},{7,15},{8,0},{9,1},... | collective-permute-start | bytes 98312 | tf_op jit(solution)/shard_map/ppermute | solution.py:458
  118.3 6.9 %collective-permute-start.15 = (bf16[128,128]{1,0:T(8,128)(2,1)S(1)}, bf16[128,128]{1,0:T(8,128)(2,1)S(1)}, u32[]{:S(2)}, u32[]{:S(2)}) collective-permute-start(bf16[128,128]{1,0:T(8,128)(2,1)S(1)} %get-tuple-element.115), channel_id=1, source_target_pairs={{0,4},{1,5},{2,6},{3,7},{4,0},{5,1},{6,2},{7,3},{8,12},{9,13},{10,... | collective-permute-start | bytes 98312 | tf_op jit(solution)/shard_map/ppermute | solution.py:458
  125.2 7.1 %copy-start.5 = (f32[256,256]{1,0:T(8,128)}, f32[256,256]{1,0:T(8,128)S(1)}, u32[]{:S(2)}) copy-start(f32[256,256]{1,0:T(8,128)S(1)} %get-tuple-element.139.refs_2_) | copy-start | bytes 786436
  125.3 7.0 %collective-permute-start.18 = (bf16[512,128]{1,0:T(8,128)(2,1)S(1)}, bf16[512,128]{1,0:T(8,128)(2,1)S(1)}, u32[]{:S(2)}, u32[]{:S(2)}) collective-permute-start(bf16[512,128]{1,0:T(8,128)(2,1)S(1)} %get-tuple-element.169), channel_id=1, source_target_pairs={{0,2},{1,3},{2,0},{3,1},{4,6},{5,7},{6,4},{7,5},{8,10},{9,11},{10,... | collective-permute-start | bytes 393224 | tf_op jit(solution)/shard_map/ppermute | solution.py:458
  132.3 0.7 copy-start.6
  132.3 5.6 %collective-permute-start.22 = (bf16[1024,128]{1,0:T(8,128)(2,1)S(1)}, bf16[1024,128]{1,0:T(8,128)(2,1)S(1)}, u32[]{:S(2)}, u32[]{:S(2)}) collective-permute-start(bf16[1024,128]{1,0:T(8,128)(2,1)S(1)} %constant_dynamic-update-slice_fusion.13.first_ref), channel_id=1, source_target_pairs={{0,1},{1,0},{2,3},{3,2},{4,5},{5,4},{6,7},{7,6},{8,9},{9,8},{10,11... | collective-permute-start | bytes 786440 | tf_op jit(solution)/shard_map/ppermute | solution.py:458
  136.1 10.8 %copy-start.12 = (f32[32,32]{1,0:T(8,128)S(1)}, f32[32,32]{1,0:T(8,128)}, u32[]{:S(2)}) copy-start(f32[32,32]{1,0:T(8,128)} %fold_groups.1) | copy-start | bytes 12292
  136.1 10.7 %collective-permute-start.21 = (f32[32,33]{1,0:T(8,128)S(1)}, f32[32,33]{1,0:T(8,128)S(1)}, u32[]{:S(2)}, u32[]{:S(2)}) collective-permute-start(f32[32,33]{1,0:T(8,128)S(1)} %pad_maximum_fusion), channel_id=1, source_target_pairs={{0,3},{1,2},{2,1},{3,0},{4,7},{5,6},{6,5},{7,4},{8,11},{9,10},{10,... | collective-permute-start | bytes 12680 | tf_op jit(solution)/shard_map/ppermute | solution.py:458
  137.0 9.8 %collective-permute-start.20 = (f32[32,33]{1,0:T(8,128)S(1)}, f32[32,33]{1,0:T(8,128)S(1)}, u32[]{:S(2)}, u32[]{:S(2)}) collective-permute-start(f32[32,33]{1,0:T(8,128)S(1)} %pad_maximum_fusion), channel_id=1, source_target_pairs={{0,2},{1,3},{2,0},{3,1},{4,6},{5,7},{6,4},{7,5},{8,10},{9,11},{10,... | collective-permute-start | bytes 12680 | tf_op jit(solution)/shard_map/ppermute | solution.py:458
  137.7 9.1 %collective-permute-start.19 = (f32[32,33]{1,0:T(8,128)S(1)}, f32[32,33]{1,0:T(8,128)S(1)}, u32[]{:S(2)}, u32[]{:S(2)}) collective-permute-start(f32[32,33]{1,0:T(8,128)S(1)} %pad_maximum_fusion), channel_id=1, source_target_pairs={{0,1},{1,0},{2,3},{3,2},{4,5},{5,4},{6,7},{7,6},{8,9},{9,8},{10,11... | collective-permute-start | bytes 12680 | tf_op jit(solution)/shard_map/ppermute | solution.py:458
  146.9 16.7 %collective-permute-start.25 = (f32[32,33]{1,0:T(8,128)S(1)}, f32[32,33]{1,0:T(8,128)S(1)}, u32[]{:S(2)}, u32[]{:S(2)}) collective-permute-start(f32[32,33]{1,0:T(8,128)S(1)} %add_add_fusion), channel_id=1, source_target_pairs={{0,12},{1,13},{2,14},{3,15},{4,8},{5,9},{6,10},{7,11},{8,4},{9,5},... | collective-permute-start | bytes 12680 | tf_op jit(solution)/shard_map/ppermute | solution.py:458
  150.5 13.1 %collective-permute-start.24 = (f32[32,33]{1,0:T(8,128)S(1)}, f32[32,33]{1,0:T(8,128)S(1)}, u32[]{:S(2)}, u32[]{:S(2)}) collective-permute-start(f32[32,33]{1,0:T(8,128)S(1)} %add_add_fusion), channel_id=1, source_target_pairs={{0,8},{1,9},{2,10},{3,11},{4,12},{5,13},{6,14},{7,15},{8,0},{9,1},... | collective-permute-start | bytes 12680 | tf_op jit(solution)/shard_map/ppermute | solution.py:458
  150.5 13.1 %collective-permute-start.23 = (f32[32,33]{1,0:T(8,128)S(1)}, f32[32,33]{1,0:T(8,128)S(1)}, u32[]{:S(2)}, u32[]{:S(2)}) collective-permute-start(f32[32,33]{1,0:T(8,128)S(1)} %add_add_fusion), channel_id=1, source_target_pairs={{0,4},{1,5},{2,6},{3,7},{4,0},{5,1},{6,2},{7,3},{8,12},{9,13},{10,... | collective-permute-start | bytes 12680 | tf_op jit(solution)/shard_map/ppermute | solution.py:458
  163.6 0.7 copy-start.13
